TPU v7x, 32 devices: a whole 2x2x4 slice. The times are simulated.
32 devices in a mesh: groups: 2 (over x), row: 8 (over z, y), col: 2 (over core).
Axes of the slice: x: 2, y: 2, z: 4, core: 2. Of those that a mesh axis runs over, the one named last changes fastest.
Arguments:
- activations: bfloat16 [1536, 28672], P(('groups', 'row'), 'col'), parts along dimension 0, may hold values from -6 to 6
- gradients: bfloat16 [1536, 8192], P(('groups', 'col'), 'row'), parts along dimension 0, may hold values from -6 to 6
- input_basis: bfloat16 [28672, 14336], P('col', 'row'), may hold values from -0.03125 to 0.03125
- output_basis: bfloat16 [8192, 4096], P('row', 'col'), may hold values from -0.0625 to 0.0625
- prior_correction: float32 [8192, 14336], P(('groups', 'col'), 'row'), parts along dimension 0, may hold values from 0.5 to 2
Outputs:
- correction: float32 [8192, 14336], P(('groups', 'col'), 'row'), parts along dimension 0
There are 2 independent parts, one for each index of `groups`. A program takes and returns all parts, laid end to end along the dimension named above; an argument that names none is the same for every part. Nothing has to cross between parts.
All inputs are finite; a program needn't handle non-finite values.
Results may differ from a plain program's by a relative error of at most 0.00036.
Values may be sent and summed in bfloat16 or wider, within the bound.
A program may use at most 256 MiB of HBM per device.

v0:
```python
import jax
import jax.numpy as jnp
from jax import lax
from jax.sharding import PartitionSpec as P

TOKENS = 768


def per_device(activations, gradients, input_basis, output_basis, prior_correction):
    partial_act = jnp.dot(
        lax.all_gather(activations, "row", axis=0, tiled=True),
        input_basis,
        preferred_element_type=jnp.float32,
    )
    proj_act = lax.psum(partial_act, "col")
    sq_act = (proj_act * proj_act).astype(jnp.bfloat16)
    grad_whole = lax.all_gather(gradients, "col", axis=0, tiled=True)
    partial_grad = jnp.dot(grad_whole, output_basis, preferred_element_type=jnp.float32)
    proj_grad = lax.psum(partial_grad, "row")
    sq_grad = (proj_grad * proj_grad).astype(jnp.bfloat16)
    increment = lax.dot_general(
        sq_grad, sq_act, (((0,), (0,)), ((), ())), preferred_element_type=jnp.float32
    )
    return prior_correction + increment / TOKENS


def solution(mesh):
    return jax.shard_map(
        per_device,
        mesh=mesh,
        in_specs=(
            P(("groups", "row"), "col"),
            P(("groups", "col"), "row"),
            P("col", "row"),
            P("row", "col"),
            P(("groups", "col"), "row"),
        ),
        out_specs=P(("groups", "col"), "row"),
        check_vma=False,
    )
```

profile of v0, /device:TPU:0, one launch (start us, length us, event | category | flops | bytes accessed | tf_op | source)
XLA Modules:
  0.0 714.2 jit_solution(9869496280016763487)
XLA Ops:
  6.5 0.0 all-gather.3.cloned.1.call-start
  6.5 0.7 all-gather.3.cloned.1.call-update
  7.3 0.0 all-gather.5.cloned.1.call-start
  7.3 0.7 all-gather.5.cloned.1.call-update
  8.0 0.0 all-reduce.3.cloned.1.call-start
  8.1 13.4 %all-gather.3.cloned.1.call-done = bf16[768,1024]{1,0:T(8,128)(2,1)} async-done(((bf16[384,1024]{1,0:T(8,128)(2,1)}), bf16[768,1024]{1,0:T(8,128)(2,1)}) %all-gather.3.cloned.1.call-update) | async-done | bytes 1572880 | tf_op jit(solution)/shard_map/all_gather | solution.py:17
  21.4 8.8 %fusion = f32[768,2048]{1,0:T(8,128)} fusion(bf16[768,1024]{1,0:T(8,128)(2,1)} %all-gather.3.cloned.1.call-done, bf16[1024,2048]{1,0:T(8,128)(2,1)} %param.8), kind=kOutput, calls=%fused_computation.3 | convolution fusion | flops 3221225472 | bytes 12058624 | tf_op jit(solution)/shard_map/dot_general | solution.py:18
  30.2 0.0 all-reduce.3.cloned.1.call-update
  30.2 0.0 all-reduce.5.cloned.1.call-start
  30.3 415.3 %all-gather.5.cloned.1.call-done = bf16[768,14336]{1,0:T(8,128)(2,1)} async-done(((bf16[96,14336]{1,0:T(8,128)(2,1)}), bf16[768,14336]{1,0:T(8,128)(2,1)}) %all-gather.5.cloned.1.call-update) | async-done | bytes 22020112 | tf_op jit(solution)/shard_map/all_gather | solution.py:11
  445.6 47.4 %fusion.1 = f32[768,1792]{1,0:T(8,128)} fusion(bf16[768,14336]{1,0:T(8,128)(2,1)} %all-gather.5.cloned.1.call-done, bf16[14336,1792]{1,0:T(8,128)(2,1)} %param.7), kind=kOutput, calls=%fused_computation.4 | convolution fusion | flops 39460012032 | bytes 78905344 | tf_op jit(solution)/shard_map/dot_general | solution.py:10
  493.0 0.0 all-reduce.5.cloned.1.call-update
  493.0 167.5 %all-reduce.3.cloned.1.call-done = f32[768,2048]{1,0:T(8,128)} async-done(((f32[768,2048]{1,0:T(8,128)}), f32[768,2048]{1,0:T(8,128)}) %all-reduce.3.cloned.1.call-update) | async-done | bytes 6291472 | tf_op jit(solution)/shard_map/psum | solution.py:19
  660.6 32.1 %all-reduce.5.cloned.1.call-done = f32[768,1792]{1,0:T(8,128)} async-done(((f32[768,1792]{1,0:T(8,128)}), f32[768,1792]{1,0:T(8,128)}) %all-reduce.5.cloned.1.call-update) | async-done | bytes 5505040 | tf_op jit(solution)/shard_map/psum | solution.py:15
  692.7 14.9 %multiply_add_fusion = f32[2048,1792]{1,0:T(8,128)} fusion(f32[2048,1792]{1,0:T(8,128)} %param.9, f32[768,2048]{1,0:T(8,128)} %all-reduce.3.cloned.1.call-done, f32[768,1792]{1,0:T(8,128)} %all-reduce.5.cloned.1.call-done), kind=kOutput, calls=%fused_computation | convolution fusion | flops 5650382848 | bytes 41156608 | tf_op jit(solution)/shard_map/dot_general | solution.py:21
Async XLA Ops:
  6.5 14.9 %all-gather.3.cloned.1.call-start = ((), (), s32[]{:S(2)}) async-start(), calls=%async_computation | async-start | bytes 2359296 | tf_op jit(solution)/shard_map/all_gather | solution.py:17
  7.3 438.4 %all-gather.5.cloned.1.call-start = ((), (), s32[]{:S(2)}) async-start(), calls=%async_computation.2 | async-start | bytes 24772608 | tf_op jit(solution)/shard_map/all_gather | solution.py:11
  8.0 652.6 %all-reduce.3.cloned.1.call-start = ((), (), s32[]{:S(2)}) async-start(), calls=%async_computation.1 | async-start | bytes 12582912 | tf_op jit(solution)/shard_map/psum | solution.py:19
  30.2 662.5 %all-reduce.5.cloned.1.call-start = ((), (), s32[]{:S(2)}) async-start(), calls=%async_computation.3 | async-start | bytes 11010048 | tf_op jit(solution)/shard_map/psum | solution.py:15
Sparse Core Ops, SparseCore 0:
  8.9 12.4 all-gather.2
  23.0 422.6 all-gather.4
  449.4 211.1 all-reduce.2
  663.1 29.5 all-reduce.4
where the time goes:
time: 714 us
  waiting for transfers between devices  630 us (88%)
  matrix products  71.1 us (10%)
  between operations  13.1 us (2%)
    all_gather x1, waiting for transfers between devices, per_device(): lax.all_gather(activations, 'row', axis=0, tiled=True)  415 us
    psum x1, waiting for transfers between devices, per_device(): proj_grad = lax.psum(partial_grad, 'row')  168 us
    dot_general x1, matrix products, per_device(): jnp.dot(lax.all_gather(activations, 'row', axis=0, tiled=True), input_bas...  47.4 us
    psum x1, waiting for transfers between devices, per_device(): proj_act = lax.psum(partial_act, 'col')  32.1 us
    dot_general x1, matrix products, per_device(): lax.dot_general(sq_grad, sq_act, (((0,), (0,)), ((), ())), preferred_elem...  14.9 us
  transfers between devices with their start and end apart: 4, of which 4 were waited for; matrix products, arithmetic and copies ran while one was open for 8% of the time, Pallas kernels for 0%

commit v1 on v0

v1 whole, which is shorter than its diff:
```python
import functools

import jax
import jax.numpy as jnp
from jax import lax
from jax.experimental import pallas as pl
from jax.experimental.pallas import tpu as pltpu
from jax.sharding import PartitionSpec as P

TOKENS = 768
CHUNK = 2048
TILE = 256
RING = 8
HOPS = RING // 2


def block_of(position):
    q = lax.rem(position + 2 * RING, RING)
    return jnp.where(q < RING // 2, 2 * q, 2 * (RING - 1 - q) + 1)


def ring_kernel(
    x, g, ib, ob, sqa, sqg,
    gathered, acc, part, sums, basis, grads, rx, stage_g, stage_a,
    ag_send, ag_recv, rs_send, rs_recv, own_sem, basis_sem, g_sem, rx_send, rx_recv, sq_send, sq_recv, out_sem,
):
    rows = x.shape[0]
    chunks = x.shape[1] // CHUNK
    half = CHUNK // 2
    tokens = acc.shape[0]
    mine = tokens // 2
    tiles = acc.shape[1] // TILE

    me = lax.axis_index("row")
    core = lax.axis_index("col")
    pos = jnp.where(lax.rem(me, 2) == 0, me // 2, RING - 1 - me // 2)
    to = ({"row": block_of(pos + 1)}, {"row": block_of(pos - 1)})
    peer = {"col": 1 - core}

    def rows_of(position):
        return pl.ds(pl.multiple_of(block_of(position) * rows, 32), rows)

    barrier = pltpu.get_barrier_semaphore()
    for other in (to[0], to[1], peer):
        pl.semaphore_signal(barrier, inc=1, device_id=other, device_id_type=pl.DeviceIdType.MESH)
    pl.semaphore_wait(barrier, 3)

    order = list(range(chunks))
    order.insert(chunks - 2, None)

    def ag(i, s, d):
        chunk = order[i]
        if s == HOPS - 1:
            start, width = d * half, half
        else:
            start, width = 0, CHUNK
        where = rows_of(pos - s if d == 0 else pos + s)
        cols = pl.ds(start, width)
        dst = sqg.at[where, cols] if chunk is None else gathered.at[chunk, where, cols]
        if s > 0:
            src = dst
        elif chunk is None:
            src = stage_g
        else:
            src = x.at[:, pl.ds(chunk * CHUNK, CHUNK)]
        return pltpu.make_async_remote_copy(
            src_ref=src, dst_ref=dst, send_sem=ag_send.at[i, s, d], recv_sem=ag_recv.at[i, s, d],
            device_id=to[d], device_id_type=pl.DeviceIdType.MESH,
        )

    def send(i, s):
        for d in range(2):
            ag(i, s, d).start()

    def recv(i, s):
        for d in range(2):
            ag(i, s, d).wait_recv()

    def rs(t, d):
        src = part.at[rows_of(pos - 1 if d == 0 else pos + 1), pl.ds(d * half, half)] if t == 0 else sums.at[t - 1, d]
        return pltpu.make_async_remote_copy(
            src_ref=src, dst_ref=sums.at[t, d], send_sem=rs_send.at[t, d], recv_sem=rs_recv.at[t, d],
            device_id=to[d], device_id_type=pl.DeviceIdType.MESH,
        )

    def rs_step(t):
        for d in range(2):
            rs(t, d).wait_recv()
            own = part[rows_of(pos - 2 - t if d == 0 else pos + 2 + t), pl.ds(d * half, half)]
            total = sums[t, d] + own
            if t < RING - 2:
                sums[t, d] = total
                rs(t + 1, d).start()
            else:
                stage_g[:, pl.ds(d * half, half)] = (total * total).astype(jnp.bfloat16)
        if t == RING - 2:
            pltpu.make_async_copy(stage_g, sqg.at[rows_of(pos), :], out_sem.at[0]).start()

    def own_copy(chunk):
        return pltpu.make_async_copy(
            x.at[:, pl.ds(chunk * CHUNK, CHUNK)], gathered.at[chunk, rows_of(pos), :], own_sem.at[chunk]
        )

    def load(chunk, h):
        return pltpu.make_async_copy(ib.at[pl.ds(chunk * CHUNK + h * half, half), :], basis.at[h], basis_sem.at[h])

    def load_ob(h):
        return pltpu.make_async_copy(
            ob.at[:, pl.ds(h * half, half)], basis.at[h, :, pl.ds(0, half)], basis_sem.at[h]
        )

    def matmul(chunk):
        own_copy(chunk).wait()
        for h in range(2):
            load(chunk, h).wait()

            @pl.loop(0, tiles)
            def _(j):
                cols = pl.ds(pl.multiple_of(j * TILE, TILE), TILE)
                acc[:, cols] += jnp.dot(
                    gathered[chunk, :, pl.ds(h * half, half)], basis[h, :, cols], preferred_element_type=jnp.float32
                )

            if chunk + 1 < chunks:
                load(chunk + 1, h).start()

    send(0, 0)
    g_rows = pl.ds(pl.multiple_of(core * mine, 32), mine)
    g_remote = pltpu.make_async_remote_copy(
        src_ref=g, dst_ref=grads.at[g_rows, :], send_sem=g_sem.at[0], recv_sem=g_sem.at[1],
        device_id=peer, device_id_type=pl.DeviceIdType.MESH,
    )
    g_local = pltpu.make_async_copy(g, grads.at[g_rows, :], g_sem.at[2])
    g_remote.start()
    g_local.start()
    for h in range(2):
        load_ob(h).start()
    for chunk in range(chunks):
        own_copy(chunk).start()

    @pl.loop(0, tiles)
    def _(j):
        acc[:, pl.ds(pl.multiple_of(j * TILE, TILE), TILE)] = jnp.zeros((tokens, TILE), jnp.float32)

    g_local.wait()
    g_remote.wait()
    for h in range(2):
        load_ob(h).wait()

        @pl.loop(0, half // TILE)
        def _(j):
            cols = pl.ds(pl.multiple_of(j * TILE, TILE), TILE)
            part[:, pl.ds(pl.multiple_of(h * half + j * TILE, TILE), TILE)] = jnp.dot(
                grads[...], basis[h, :, cols], preferred_element_type=jnp.float32
            )

        load(0, h).start()
        rs(0, h).start()
    recv(0, 0)
    send(0, 1)

    last = len(order) - 1
    for i in range(last + 1):
        if i < last:
            send(i + 1, 0)
        recv(i, 1)
        send(i, 2)
        if 2 * i < RING - 1:
            rs_step(2 * i)
        if i < last:
            recv(i + 1, 0)
            send(i + 1, 1)
        recv(i, 2)
        send(i, 3)
        if 2 * i + 1 < RING - 1:
            rs_step(2 * i + 1)
        if i > 0:
            recv(i - 1, 3)
            if order[i - 1] is not None:
                matmul(order[i - 1])
    recv(last, 3)
    chunk = order[last]

    theirs = pl.ds(pl.multiple_of((1 - core) * mine, 32), mine)
    own_copy(chunk).wait()
    for h in range(2):
        load(chunk, h).wait()

    def swap(j):
        cols = pl.ds(pl.multiple_of(j * TILE, TILE), TILE)
        return pltpu.make_async_remote_copy(
            src_ref=acc.at[theirs, cols], dst_ref=rx.at[j], send_sem=rx_send.at[j], recv_sem=rx_recv.at[j],
            device_id=peer, device_id_type=pl.DeviceIdType.MESH,
        )

    def finish(j):
        cols = pl.ds(pl.multiple_of(j * TILE, TILE), TILE)
        return (
            pltpu.make_async_remote_copy(
                src_ref=stage_a.at[j], dst_ref=sqa.at[g_rows, cols], send_sem=sq_send.at[j], recv_sem=sq_recv.at[j],
                device_id=peer, device_id_type=pl.DeviceIdType.MESH,
            ),
            pltpu.make_async_copy(stage_a.at[j], sqa.at[g_rows, cols], out_sem.at[1 + j]),
        )

    @pl.loop(0, tiles)
    def _(j):
        cols = pl.ds(pl.multiple_of(j * TILE, TILE), TILE)
        total = acc[:, cols]
        for h in range(2):
            total += jnp.dot(
                gathered[chunk, :, pl.ds(h * half, half)], basis[h, :, cols], preferred_element_type=jnp.float32
            )
        acc[:, cols] = total
        swap(j).start()

    @pl.loop(0, tiles)
    def _(j):
        cols = pl.ds(pl.multiple_of(j * TILE, TILE), TILE)
        swap(j).wait_recv()
        total = acc[g_rows, cols] + rx[j]
        stage_a[j] = (total * total).astype(jnp.bfloat16)
        for copy in finish(j):
            copy.start()

    @pl.loop(0, tiles)
    def _(j):
        swap(j).wait_send()
        for copy in finish(j):
            copy.wait()

    pltpu.make_async_copy(stage_g, sqg.at[rows_of(pos), :], out_sem.at[0]).wait()
    for i in range(last + 1):
        for s in range(HOPS):
            for d in range(2):
                ag(i, s, d).wait_send()
    for t in range(RING - 1):
        for d in range(2):
            rs(t, d).wait_send()


def squares(activations, gradients, input_basis, output_basis):
    rows, width = activations.shape
    tokens = rows * RING
    columns = input_basis.shape[1]
    chunks, half, tiles = width // CHUNK, CHUNK // 2, columns // TILE
    any_spec = pl.BlockSpec(memory_space=pl.ANY)
    dma = pltpu.SemaphoreType.DMA
    return pl.pallas_call(
        ring_kernel,
        out_shape=(
            jax.ShapeDtypeStruct((tokens, columns), jnp.bfloat16),
            jax.ShapeDtypeStruct((tokens, CHUNK), jnp.bfloat16),
        ),
        in_specs=[any_spec] * 4,
        out_specs=(any_spec, any_spec),
        scratch_shapes=[
            pltpu.VMEM((chunks, tokens, CHUNK), jnp.bfloat16),
            pltpu.VMEM((tokens, columns), jnp.float32),
            pltpu.VMEM((tokens, CHUNK), jnp.float32),
            pltpu.VMEM((RING - 1, 2, rows, half), jnp.float32),
            pltpu.VMEM((2, half, columns), jnp.bfloat16),
            pltpu.VMEM((tokens, half), jnp.bfloat16),
            pltpu.VMEM((tiles, tokens // 2, TILE), jnp.float32),
            pltpu.VMEM((rows, CHUNK), jnp.bfloat16),
            pltpu.VMEM((tiles, tokens // 2, TILE), jnp.bfloat16),
            dma((chunks + 1, HOPS, 2)),
            dma((chunks + 1, HOPS, 2)),
            dma((RING - 1, 2)),
            dma((RING - 1, 2)),
            dma((chunks,)),
            dma((2,)),
            dma((3,)),
            dma((tiles,)),
            dma((tiles,)),
            dma((tiles,)),
            dma((tiles,)),
            dma((tiles + 1,)),
        ],
        compiler_params=pltpu.CompilerParams(
            collective_id=0, has_side_effects=True, vmem_limit_bytes=60 * 2**20
        ),
        cost_estimate=pl.CostEstimate(
            flops=2 * tokens * (width * columns + half * CHUNK),
            bytes_accessed=2 * (width * columns + half * CHUNK + tokens * (columns + CHUNK)),
            transcendentals=0,
        ),
    )(activations, gradients, input_basis, output_basis)


def squares_by_collectives(activations, gradients, input_basis, output_basis):
    partial_act = jnp.dot(
        lax.all_gather(activations, "row", axis=0, tiled=True),
        input_basis,
        preferred_element_type=jnp.float32,
    )
    proj_act = lax.psum(partial_act, "col")
    grad_whole = lax.all_gather(gradients, "col", axis=0, tiled=True)
    partial_grad = jnp.dot(grad_whole, output_basis, preferred_element_type=jnp.float32)
    proj_grad = lax.psum(partial_grad, "row")
    return (proj_act * proj_act).astype(jnp.bfloat16), (proj_grad * proj_grad).astype(jnp.bfloat16)


def per_device(ring, activations, gradients, input_basis, output_basis, prior_correction):
    form = squares if ring else squares_by_collectives
    sq_act, sq_grad = form(activations, gradients, input_basis, output_basis)
    increment = lax.dot_general(
        sq_grad, sq_act, (((0,), (0,)), ((), ())), preferred_element_type=jnp.float32
    )
    return prior_correction + increment / TOKENS


def solution(mesh):
    ring = mesh.shape["row"] == RING and mesh.shape["col"] == 2
    return jax.shard_map(
        functools.partial(per_device, ring),
        mesh=mesh,
        in_specs=(
            P(("groups", "row"), "col"),
            P(("groups", "col"), "row"),
            P("col", "row"),
            P("row", "col"),
            P(("groups", "col"), "row"),
        ),
        out_specs=P(("groups", "col"), "row"),
        check_vma=False,
    )
```

time: 714 us -> 332 us (0.46)
  waiting for transfers between devices: 630 us -> 0 us
  Pallas kernels: 0 us -> 318 us
  matrix products: 71.1 us -> 13.6 us
  between operations: 13.1 us -> 0.01 us
    all_gather x2 -> x0, waiting for transfers between devices: 429 us -> none  [the longest x1 415 us: per_device(): lax.all_gather(activations, 'row', axis=0, tiled=True)]
    pallas_call x0 -> x1, Pallas kernels: none -> 318 us  [squares(): pl.pallas_call(ring_kernel, out_shape=(jax.ShapeDtypeStruct((tokens, colu...]
    psum x2 -> x0, waiting for transfers between devices: 200 us -> none  [the longest x1 168 us: per_device(): proj_grad = lax.psum(partial_grad, 'row')]
    dot_general x2 -> x0, matrix products: 56.2 us -> none  [the longest x1 47.4 us: per_device(): jnp.dot(lax.all_gather(activations, 'row', axis=0, tiled=True), input_bas...]
  transfers between devices with their start and end apart: 4 -> 0, of which waited for: 4 -> 0; matrix products, arithmetic and copies ran while one was open for 8% -> 0% of each run, Pallas kernels for 0% -> 0%
where the time goes in v1:
time: 332 us
  Pallas kernels  318 us (96%)
  matrix products  13.6 us (4%)
    pallas_call x1, Pallas kernels, squares(): pl.pallas_call(ring_kernel, out_shape=(jax.ShapeDtypeStruct((tokens, colu...  318 us
    dot_general x1, matrix products, per_device(): lax.dot_general(sq_grad, sq_act, (((0,), (0,)), ((), ())), preferred_elem...  13.6 us

profile of v1, /device:TPU:0, one launch (start us, length us, event | category | flops | bytes accessed | tf_op | source)
XLA Modules:
  0.0 331.7 jit_solution(1999758668606402162)
XLA Ops:
  0.0 318.1 %shard_map.55 = (bf16[768,1792]{1,0:T(8,128)(2,1)}, bf16[768,2048]{1,0:T(8,128)(2,1)}) custom-call(bf16[96,14336]{1,0:T(8,128)(2,1)} %x.1, bf16[384,1024]{1,0:T(8,128)(2,1)} %g.1, bf16[14336,1792]{1,0:T(8,128)(2,1)} %ib.1, bf16[1024,2048]{1,0:T(8,128)(2,1)} %ob.1), custom_call_target="tpu_custom_call" | custom-call | flops 42681237504 | bytes 61472768 | tf_op jit(solution)/shard_map/pallas_call | solution.py:249
  318.1 13.6 %multiply_add_fusion = f32[2048,1792]{1,0:T(8,128)} fusion(f32[2048,1792]{1,0:T(8,128)} %param.9, bf16[768,2048]{1,0:T(8,128)(2,1)} %get-tuple-element.7, bf16[768,1792]{1,0:T(8,128)(2,1)} %get-tuple-element.8), kind=kOutput, calls=%fused_computation | convolution fusion | flops 5644484608 | bytes 35258368 | tf_op jit(solution)/shard_map/dot_general | solution.py:307

commit v2 on v1

--- a/solution.py
+++ b/solution.py
@@ -46,7 +46,7 @@
     pl.semaphore_wait(barrier, 3)
 
     order = list(range(chunks))
-    order.insert(chunks - 2, None)
+    order.append(None)
 
     def ag(i, s, d):
         chunk = order[i]
@@ -156,12 +156,13 @@
 
         load(0, h).start()
         rs(0, h).start()
+    send(1, 0)
     recv(0, 0)
     send(0, 1)
 
     last = len(order) - 1
     for i in range(last + 1):
-        if i < last:
+        if 0 < i < last:
             send(i + 1, 0)
         recv(i, 1)
         send(i, 2)
@@ -176,10 +177,9 @@
             rs_step(2 * i + 1)
         if i > 0:
             recv(i - 1, 3)
-            if order[i - 1] is not None:
+            if i < last:
                 matmul(order[i - 1])
-    recv(last, 3)
-    chunk = order[last]
+    chunk = order[last - 1]
 
     theirs = pl.ds(pl.multiple_of((1 - core) * mine, 32), mine)
     own_copy(chunk).wait()
@@ -229,6 +229,7 @@
         for copy in finish(j):
             copy.wait()
 
+    recv(last, 3)
     pltpu.make_async_copy(stage_g, sqg.at[rows_of(pos), :], out_sem.at[0]).wait()
     for i in range(last + 1):
         for s in range(HOPS):

time: 332 us -> 324 us (0.976)
  Pallas kernels: 318 us -> 310 us
    pallas_call x1, Pallas kernels: 318 us -> 310 us  [squares(): pl.pallas_call(ring_kernel, out_shape=(jax.ShapeDtypeStruct((tokens, colu...]
where the time goes in v2:
time: 324 us
  Pallas kernels  310 us (96%)
  matrix products  13.6 us (4%)
    pallas_call x1, Pallas kernels, squares(): pl.pallas_call(ring_kernel, out_shape=(jax.ShapeDtypeStruct((tokens, colu...  310 us
    dot_general x1, matrix products, per_device(): lax.dot_general(sq_grad, sq_act, (((0,), (0,)), ((), ())), preferred_elem...  13.6 us

profile of v2, /device:TPU:0, one launch (start us, length us, event | category | flops | bytes accessed | tf_op | source)
XLA Modules:
  0.0 323.5 jit_solution(15631995206904659659)
XLA Ops:
  0.0 309.9 %shard_map.55 = (bf16[768,1792]{1,0:T(8,128)(2,1)}, bf16[768,2048]{1,0:T(8,128)(2,1)}) custom-call(bf16[96,14336]{1,0:T(8,128)(2,1)} %x.1, bf16[384,1024]{1,0:T(8,128)(2,1)} %g.1, bf16[14336,1792]{1,0:T(8,128)(2,1)} %ib.1, bf16[1024,2048]{1,0:T(8,128)(2,1)} %ob.1), custom_call_target="tpu_custom_call" | custom-call | flops 42681237504 | bytes 61472768 | tf_op jit(solution)/shard_map/pallas_call | solution.py:250
  309.9 13.6 %multiply_add_fusion = f32[2048,1792]{1,0:T(8,128)} fusion(f32[2048,1792]{1,0:T(8,128)} %param.9, bf16[768,2048]{1,0:T(8,128)(2,1)} %get-tuple-element.7, bf16[768,1792]{1,0:T(8,128)(2,1)} %get-tuple-element.8), kind=kOutput, calls=%fused_computation | convolution fusion | flops 5644484608 | bytes 35258368 | tf_op jit(solution)/shard_map/dot_general | solution.py:308
